TPU v7x, 32 devices: a whole 2x2x4 slice. The times are simulated.
32 devices in a mesh: groups: 2 (over x), rows: 16 (over z, y, core).
Axes of the slice: x: 2, y: 2, z: 4, core: 2. Of those that a mesh axis runs over, the one named last changes fastest.
Arguments:
- image_query: bfloat16 [12288, 2048], P(('groups', 'rows')), parts along dimension 0, may hold values from -40 to 40
- image_pairs: bfloat16 [2, 12288, 2048], P(None, ('groups', 'rows')), parts along dimension 1, may hold values from -6 to 6
- text_query: bfloat16 [512, 2048], P(('groups', 'rows')), parts along dimension 0, may hold values from -40 to 40
- text_pairs: bfloat16 [2, 512, 2048], P(None, ('groups', 'rows')), parts along dimension 1, may hold values from -6 to 6
- text_mask: int32 [512], P('groups'), parts along dimension 0, may hold values 0 or 1
- window_offsets: int32 [16, 2], replicated, may hold values from -1 to 1, as said below
- timestep: int32 [1], replicated, may hold values from 0 to 49
- gate_table: float32 [50, 2, 2048], replicated, may hold values from 0.5 to 2
Outputs:
- image_out: bfloat16 [12288, 2048], P(('groups', 'rows')), parts along dimension 0
- text_out: bfloat16 [512, 2048], P(('groups', 'rows')), parts along dimension 0
There are 2 independent parts, one for each index of `groups`. A program takes and returns all parts, laid end to end along the dimension named above; an argument that names none is the same for every part. Nothing has to cross between parts.
Inputs may be any that keep to these rules, and one draw needn't show every extreme that they name: window_offsets[h, 0] is -1 or 0 and window_offsets[h, 1] is 0 or 1; some head has -1 and some head has 1.
All inputs are finite; a program needn't handle non-finite values.
Results may differ from a plain program's by a relative error of at most 0.02.
Values may be sent and summed in bfloat16 or wider, within the bound.
A program may use at most 128 MiB of HBM per device.

v0:
```python
import math
import jax
import jax.numpy as jnp
from jax import lax
from jax.sharding import PartitionSpec as P

TILE = 384
masked_score = -1e30


def extended_2(cells, sides, width):
    for axis, dim in sides:
        count = lax.axis_size(axis)
        ends = count - 1
        head = lax.slice_in_dim(cells, 0, width, axis=dim)
        tail = lax.slice_in_dim(cells, cells.shape[dim] - width, cells.shape[dim], axis=dim)
        cells = jnp.concatenate(
            [
                lax.ppermute(tail, axis, [(i, (i + 1) % count) for i in range(ends)]),
                cells,
                lax.ppermute(head, axis, [((i + 1) % count, i) for i in range(ends)]),
            ],
            axis=dim,
        )
    return cells


def attend_tiles(queries, key_rows, value_rows, allowed, scaling):
    scores = (
        jnp.einsum("tqhe,tkhe->tqhk", queries, key_rows, preferred_element_type=jnp.float32)
        * scaling
    )
    scores = jnp.where(allowed, scores, masked_score)
    maxima = jnp.max(scores, axis=-1)
    exponent = jnp.where(allowed, jnp.exp(scores - maxima[..., None]), 0.0)
    totals = jnp.sum(exponent, axis=-1)
    summed = jnp.einsum(
        "tqhk,tkhe->tqhe",
        exponent.astype(jnp.bfloat16),
        value_rows,
        preferred_element_type=jnp.float32,
    )
    return (maxima, totals, summed.astype(jnp.bfloat16))


def attend_rows(queries, key_rows, value_rows, allowed, scaling):
    scores = (
        jnp.einsum("qhe,khe->qhk", queries, key_rows, preferred_element_type=jnp.float32) * scaling
    )
    scores = jnp.where(allowed, scores, masked_score)
    maxima = jnp.max(scores, axis=-1)
    exponent = jnp.where(allowed, jnp.exp(scores - maxima[..., None]), 0.0)
    totals = jnp.sum(exponent, axis=-1)
    summed = jnp.einsum(
        "qhk,khe->qhe",
        exponent.astype(jnp.bfloat16),
        value_rows,
        preferred_element_type=jnp.float32,
    )
    return (maxima, totals, summed.astype(jnp.bfloat16))


def combine_groups(groups):
    largest = groups[0][0]
    for member in groups[1:]:
        largest = jnp.maximum(largest, member[0])
    totals = 0.0
    summed = 0.0
    for member in groups:
        factor = jnp.exp(member[0] - largest)
        totals = totals + member[1] * factor
        summed = summed + member[2].astype(jnp.float32) * factor[..., None]
    return summed / totals[..., None]


def on_device(
    image_query,
    image_pairs,
    text_query,
    text_pairs,
    text_mask,
    window_offsets,
    timestep,
    gate_table,
):
    rows_dev, width = image_query.shape
    tiles_dev = rows_dev // TILE
    head_count = window_offsets.shape[0]
    head_width = width // head_count
    scaling = 1.0 / math.sqrt(head_width)
    position = lax.axis_index("rows")
    tiles_all = tiles_dev * lax.axis_size("rows")
    first_tile = position * tiles_dev
    reach_back = window_offsets[:, 0]
    reach_ahead = window_offsets[:, 1]
    text_queries, text_gathered = (
        lax.all_gather(text_query, "rows", axis=0, tiled=True),
        lax.all_gather(text_pairs, "rows", axis=1, tiled=True),
    )
    text_keys = text_gathered[0].reshape(-1, head_count, head_width)
    text_values = text_gathered[1].reshape(-1, head_count, head_width)
    text_allowed = (text_mask == 1)[None, None, :]
    queries = image_query.reshape(tiles_dev, TILE, head_count, head_width)
    local_keys = image_pairs[0].reshape(tiles_dev, TILE, head_count, head_width)
    local_values = image_pairs[1].reshape(tiles_dev, TILE, head_count, head_width)

    def permitted(offset):
        target = first_tile + jnp.arange(tiles_dev, dtype=jnp.int32) + offset
        inside = (target >= 0) & (target < tiles_all)
        within = (reach_back <= offset) & (offset <= reach_ahead)
        return (inside[:, None] & within[None, :])[:, None, :, None]

    flat_queries = image_query.reshape(rows_dev, head_count, head_width)
    text_group = attend_rows(flat_queries, text_keys, text_values, text_allowed, scaling)
    text_group = (
        text_group[0].reshape(tiles_dev, TILE, head_count),
        text_group[1].reshape(tiles_dev, TILE, head_count),
        text_group[2].reshape(tiles_dev, TILE, head_count, head_width),
    )
    groups = [attend_tiles(queries, local_keys, local_values, permitted(0), scaling), text_group]
    extended = extended_2(image_pairs, (("rows", 1),), TILE)
    extended = extended.reshape(2, tiles_dev + 2, TILE, head_count, head_width)
    for offset in (-1, 1):
        groups.append(
            attend_tiles(
                queries,
                extended[0, 1 + offset : 1 + offset + tiles_dev],
                extended[1, 1 + offset : 1 + offset + tiles_dev],
                permitted(offset),
                scaling,
            )
        )
    gate_rows = lax.dynamic_index_in_dim(gate_table, timestep[0], 0, keepdims=False)
    attended = combine_groups(groups).reshape(rows_dev, width)
    image_out = (attended * gate_rows[0]).astype(jnp.bfloat16)
    text_flat = text_queries.reshape(-1, head_count, head_width)
    image_keys = image_pairs[0].reshape(rows_dev, head_count, head_width)
    image_values = image_pairs[1].reshape(rows_dev, head_count, head_width)
    every_key = jnp.ones((1, 1, rows_dev), dtype=bool)
    maxima, totals, summed = attend_rows(text_flat, image_keys, image_values, every_key, scaling)
    text_dev = text_query.shape[0]
    text_start = position * text_dev
    global_max = lax.pmax(maxima, "rows")
    factor = jnp.exp(maxima - global_max)
    scaled_summed = summed.astype(jnp.float32) * factor[..., None]
    scaled_totals = totals * factor
    whole_summed, whole_totals = lax.psum((scaled_summed, scaled_totals), "rows")
    shared_summed = lax.dynamic_slice_in_dim(whole_summed, text_start, text_dev, 0)
    shared_totals = lax.dynamic_slice_in_dim(whole_totals, text_start, text_dev, 0)
    remote = (
        lax.dynamic_slice_in_dim(global_max, text_start, text_dev, 0),
        shared_totals,
        shared_summed,
    )
    own_rows = text_query.reshape(text_dev, head_count, head_width)
    own_text = attend_rows(own_rows, text_keys, text_values, text_allowed, scaling)
    text_attended = combine_groups([remote, own_text]).reshape(text_dev, width)
    text_out = (text_attended * gate_rows[1]).astype(jnp.bfloat16)
    return (image_out, text_out)


def solution(mesh):
    placed = (
        P(("groups", "rows"), None),
        P(None, ("groups", "rows"), None),
        P(("groups", "rows"), None),
        P(None, ("groups", "rows"), None),
        P("groups"),
        P(),
        P(),
        P(),
    )
    return jax.shard_map(
        on_device,
        mesh=mesh,
        in_specs=placed,
        out_specs=(P(("groups", "rows"), None), P(("groups", "rows"), None)),
        check_vma=False,
    )
```

profile of v0, /device:TPU:0, one launch (start us, length us, event | category | flops | bytes accessed | tf_op | source)
XLA Modules:
  0.0 297.9 jit_solution(4161448792035331032)
XLA Ops:
  7.2 0.0 copy-start
  7.2 0.0 all-gather.5.cloned.1.call-start
  7.2 0.7 all-gather.5.cloned.1.call-update
  7.9 0.0 all-gather.3.cloned.1.call-start
  8.0 4.0 %collective-permute-start = (bf16[2,384,2048]{2,1,0:T(8,128)(2,1)}, bf16[2,384,2048]{2,1,0:T(8,128)(2,1)}, u32[]{:S(2)}, u32[]{:S(2)}) collective-permute-start(bf16[2,384,2048]{2,1,0:T(8,128)(2,1)} %param.9), channel_id=1, source_target_pairs={{0,1},{1,2},{2,3},{3,4},{4,5},{5,6},{6,7},{7,8},{8,9},{9,10},{10,1... | collective-permute-start | bytes 9437192 | tf_op jit(solution)/shard_map/ppermute | solution.py:19
  12.0 1.3 collective-permute-start.1
  13.3 1.7 copy.59
  15.0 0.0 all-gather.3.cloned.1.call-update
  15.0 0.0 all-reduce.2.cloned.1.call-start
  15.7 0.8 constant_dynamic-slice_fusion.1
  16.5 0.8 and_bitcast_fusion.1
  17.3 4.1 %fusion.134 = (bf16[1,384,2048]{2,1,0:T(8,128)(2,1)}, bf16[1,384,2048]{2,1,0:T(8,128)(2,1)}) fusion(bf16[2,384,2048]{2,1,0:T(8,128)(2,1)} %param.9), kind=kLoop, calls=%fused_computation.155 | loop fusion | bytes 6291456 | tf_op jit(solution)/shard_map/slice | solution.py:104
  21.4 1.9 copy.95
  23.2 2.6 copy.57
  25.8 2.5 bitcast_reduce_fusion.2
  28.3 3.6 %copy-done.2 = f32[16,384,384]{2,1,0:T(8,128)} copy-done((f32[16,384,384]{2,1,0:T(8,128)}, f32[16,384,384]{2,1,0:T(8,128)S(1)}, u32[]{:S(2)}) %copy-start.2) | copy-done | bytes 9437208
  31.9 3.5 %fusion.67 = bf16[16,384,128]{1,2,0:T(8,128)(2,1)} fusion(bf16[384,16,128]{0,2,1:T(8,128)(2,1)S(1)} %bitcast.291, f32[16,384,384]{2,1,0:T(8,128)S(1)} %get-tuple-element.26, f32[384,16]{0,1:T(8,128)S(1)} %get-tuple-element.25, pred[16]{0:T(512)(128)(4,1)S(1)} %get-tuple-element.24), kind=kOutput, calls=%fused_computation.81 | convolution fusion | flops 616562688 | bytes 12607504 | tf_op jit(solution)/shard_map/tqhk,tkhe->tqhe/dot_general | solution.py:37
  35.5 28.8 %all-gather.5.cloned.1.call-done = bf16[256,2048]{1,0:T(8,128)(2,1)} async-done(((bf16[16,2048]{1,0:T(8,128)(2,1)}), bf16[256,2048]{1,0:T(8,128)(2,1)}) %all-gather.5.cloned.1.call-update) | async-done | bytes 1048592 | tf_op jit(solution)/shard_map/all_gather | solution.py:97
  64.3 2.3 copy.74
  66.7 4.9 %bitcast_reduce_fusion.3 = (f32[256,16]{0,1:T(8,128)S(1)}, f32[16,384,256]{2,1,0:T(8,128)}) fusion(bf16[384,16,128]{0,2,1:T(8,128)(2,1)S(1)} %bitcast.287, bf16[256,16,128]{0,2,1:T(8,128)(2,1)} %bitcast.294), kind=kOutput, calls=%fused_computation.23 | convolution fusion | flops 405794816 | bytes 8929280 | tf_op jit(solution)/shard_map/qhe,khe->qhk/dot_general | solution.py:48
  71.6 66.7 %pmax.7 = f32[256,16]{0,1:T(8,128)S(1)} all-reduce(f32[256,16]{0,1:T(8,128)S(1)} %get-tuple-element.35), channel_id=1, replica_groups=mesh['groups'=2,'rows'=16] {'rows'}, use_global_device_ids=true, to_apply=%region_9.10 | all-reduce | flops 4096 | bytes 32768 | tf_op jit(solution)/shard_map/pmax | solution.py:143
  138.3 4.0 %fusion.15 = f32[256,16]{0,1:T(8,128)S(1)} fusion(f32[16,384,256]{2,1,0:T(8,128)} %get-tuple-element.36, f32[256,16]{0,1:T(8,128)S(1)} %get-tuple-element.35), kind=kLoop, calls=%fused_computation.30 | loop fusion | flops 4714496 | bytes 6324224 | tf_op jit(solution)/shard_map/reduce_sum | solution.py:53
  142.3 0.6 copy-done.1
  142.9 4.4 %bitcast_multiply_fusion.2 = f32[256,16,128]{2,0,1:T(8,128)} fusion(bf16[384,16,128]{0,2,1:T(8,128)(2,1)} %bitcast.290, f32[16,384,256]{2,1,0:T(8,128)S(1)} %copy-done.1, f32[256,16]{0,1:T(8,128)S(1)} %get-tuple-element.35, f32[256,16]{0,1:T(8,128)S(1)} %get-tuple-element.6), kind=kOutput, calls=%fused_computation.79 | convolution fusion | flops 408944640 | bytes 9994240 | tf_op jit(solution)/shard_map/qhk,khe->qhe/dot_general | solution.py:54
  147.3 0.0 all-reduce.2.cloned.1.call-update
  147.3 58.2 %psum.15 = f32[256,16]{0,1:T(8,128)S(1)} all-reduce(f32[256,16]{0,1:T(8,128)S(1)} %get-tuple-element.5), channel_id=1, replica_groups=mesh['groups'=2,'rows'=16] {'rows'}, use_global_device_ids=true, to_apply=%region_13.14 | all-reduce | flops 4096 | bytes 32768 | tf_op jit(solution)/shard_map/psum | solution.py:147
  205.5 0.0 collective-permute-done
  205.5 0.0 collective-permute-done.1
  205.5 7.6 %pad_maximum_fusion = bf16[2,1152,2048]{2,1,0:T(8,128)(2,1)} fusion(bf16[2,384,2048]{2,1,0:T(8,128)(2,1)} %collective-permute-done.1, bf16[2,384,2048]{2,1,0:T(8,128)(2,1)} %param.9, bf16[2,384,2048]{2,1,0:T(8,128)(2,1)} %collective-permute-done), kind=kLoop, calls=%fused_computation | loop fusion | flops 28311552 | bytes 18874368 | tf_op jit(solution)/shard_map/concatenate | solution.py:17
  213.1 11.0 %copy.104 = bf16[288,8,16,128]{3,2,1,0:T(8,128)(2,1)} copy(bf16[288,8,16,128]{3,1,2,0:T(8,128)(2,1)} %bitcast.284) | data formatting | bytes 18874368
  224.2 5.6 %fusion.133 = (bf16[1,1,384,16,128]{4,3,2,1,0:T(8,128)(2,1)}, bf16[1,1,384,16,128]{4,3,2,1,0:T(8,128)(2,1)}, bf16[1,1,384,16,128]{4,3,2,1,0:T(8,128)(2,1)}, bf16[1,1,384,16,128]{4,3,2,1,0:T(8,128)(2,1)S(1)}) fusion(bf16[2,3,384,16,128]{4,3,2,1,0:T(8,128)(2,1)} %bitcast.285), kind=kLoop, calls=%fused_computation.154 | loop fusion | bytes 12582912 | tf_op jit(solution)/shard_map/slice | solution.py:128
  229.8 2.8 copy.99
  232.6 2.0 copy.100
  234.6 3.3 %bitcast_reduce_fusion = (f32[384,16]{0,1:T(8,128)S(1)}, f32[16,384,384]{2,1,0:T(8,128)S(1)}) fusion(pred[16]{0:T(512)(128)(4,1)S(1)} %get-tuple-element.23, bf16[1,1,384,16,128]{4,3,2,1,0:T(8,128)(2,1)} %get-tuple-element.13, bf16[384,2048]{1,0:T(8,128)(2,1)S(1)} %copy-done), kind=kOutput, calls=%fused_computation.2 | convolution fusion | flops 611051520 | bytes 12607504 | tf_op jit(solution)/shard_map/tqhe,tkhe->tqhk/dot_general | solution.py:30
  237.9 0.0 copy-start.7
  237.9 2.7 fusion.10
  240.6 0.0 copy-done.7
  240.6 0.0 copy-start.5
  240.6 0.0 slice-start
  240.6 0.0 slice-start.1
  240.6 3.5 %fusion.73 = bf16[16,128,384]{2,1,0:T(8,128)(2,1)} fusion(f32[16,384,384]{2,1,0:T(8,128)S(1)} %get-tuple-element.28, f32[384,16]{0,1:T(8,128)S(1)} %get-tuple-element.27, pred[16]{0:T(512)(128)(4,1)S(1)} %get-tuple-element.23, bf16[1,1,384,16,128]{2,4,3,1,0:T(8,128)(2,1)S(1)} %copy-done.7), kind=kOutput, calls=%fused_computation.83 | convolution fusion | flops 616562688 | bytes 12607504 | tf_op jit(solution)/shard_map/tqhk,tkhe->tqhe/dot_general | solution.py:37
  244.1 1.9 bitcast_reduce_fusion.1
  246.1 0.3 slice-done.2
  246.3 5.5 %fusion.6 = (f32[384,16]{0,1:T(8,128)S(1)}, f32[384,16]{0,1:T(8,128)S(1)}) fusion(f32[16,384,384]{2,1,0:T(8,128)S(1)} %bitcast.283, f32[384,16]{0,1:T(8,128)S(1)} %get-tuple-element.25, pred[16]{0:T(512)(128)(4,1)S(1)} %get-tuple-element.24, f32[384,16]{0,1:T(8,128)S(1)} %get-tuple-element.29, f32[16,384,384]{2,1,0:T(8,128)S(1)} %get-tuple-element.30, ...), kind=kLoop, calls=%fused_computation.16 | loop fusion | flops 23580672 | bytes 18972704 | tf_op jit(solution)/shard_map/reduce_sum | solution.py:36
  251.8 0.0 copy-done.6
  251.8 3.5 %fusion.70 = bf16[16,128,384]{2,1,0:T(8,128)(2,1)} fusion(f32[16,384,384]{2,1,0:T(8,128)S(1)} %get-tuple-element.30, f32[384,16]{0,1:T(8,128)S(1)} %get-tuple-element.29, pred[16]{0:T(512)(128)(4,1)S(1)} %get-tuple-element.22, bf16[1,1,384,16,128]{2,4,3,1,0:T(8,128)(2,1)S(1)} %copy-done.6), kind=kOutput, calls=%fused_computation.82 | convolution fusion | flops 616562688 | bytes 12607504 | tf_op jit(solution)/shard_map/tqhk,tkhe->tqhe/dot_general | solution.py:37
  255.4 6.8 %fusion.135 = (bf16[1,256,2048]{2,0,1:T(2,128)(2,1)}, bf16[1,256,2048]{2,0,1:T(2,128)(2,1)}) fusion(bf16[2,256,2048]{2,0,1:T(2,128)(2,1)} %all-gather.3.cloned.1.call-done), kind=kLoop, calls=%fused_computation.156 | loop fusion | bytes 4194304 | tf_op jit(solution)/shard_map/slice | solution.py:101
  262.2 5.8 %copy.67 = bf16[1,256,2048]{1,2,0:T(8,128)(2,1)} copy(bf16[1,256,2048]{2,0,1:T(2,128)(2,1)} %get-tuple-element.18) | data formatting | bytes 2097152 | tf_op jit(solution)/shard_map/slice | solution.py:101
  268.0 4.8 %copy.96 = bf16[1,256,2048]{1,2,0:T(8,128)(2,1)S(1)} copy(bf16[1,256,2048]{2,0,1:T(2,128)(2,1)} %get-tuple-element.19) | data formatting | bytes 2097152
  272.7 1.4 bitcast_reduce_fusion.4
  274.2 0.0 copy-start.11
  274.2 0.0 copy-start.12
  274.2 1.7 fusion.44
  276.0 0.4 copy-done.11
  276.4 0.5 copy-done.12
  276.9 4.5 %fusion.52 = f32[1,384,16,128]{1,3,2,0:T(8,128)} fusion(bf16[16,384,128]{1,2,0:T(8,128)(2,1)S(1)} %copy-done.10, bf16[16,128,384]{2,1,0:T(8,128)(2,1)S(1)} %copy-done.11, bf16[16,128,384]{2,1,0:T(8,128)(2,1)S(1)} %copy-done.12, f32[384,16]{0,1:T(8,128)S(1)} %get-tuple-element.7, f32[384,16]{0,1:T(8,128)S(1)} %get-tuple-element.11, ...), kind=kOutput, calls=%fused_computation.63 | convolution fusion | flops 420741120 | bytes 15352064 | tf_op jit(solution)/shard_map/qhk,khe->qhe/dot_general | solution.py:54
  281.4 3.6 %copy.73 = f32[384,2048]{1,0:T(8,128)} copy(f32[384,2048]{0,1:T(8,128)} %bitcast.295) | data formatting | bytes 6291456 | tf_op jit(solution)/shard_map/reshape | solution.py:134
  285.0 0.3 fusion.136
  285.3 0.2 fusion.105
  285.5 0.1 multiply_add_fusion.1
  285.6 0.0 all-reduce.2.cloned.1.call-done
  285.7 1.7 fusion.98
  287.3 0.7 fusion.108
  288.0 3.4 %multiply_convert_fusion = bf16[384,2048]{1,0:T(8,128)(2,1)} fusion(f32[384,2048]{1,0:T(8,128)} %copy.73, f32[2048]{0:T(1024)S(1)} %bitcast.296), kind=kLoop, calls=%fused_computation.72 | loop fusion | flops 1572864 | bytes 4726784 | tf_op jit(solution)/shard_map/convert_element_type | solution.py:135
  (23 shorter events, 0.1 us)
Async XLA Ops:
  7.2 18.7 %copy-start = (bf16[384,2048]{1,0:T(8,128)(2,1)S(1)}, bf16[384,2048]{1,0:T(8,128)(2,1)}, u32[]{:S(2)}) copy-start(bf16[384,2048]{1,0:T(8,128)(2,1)} %param.8) | copy-start | bytes 4718596
  7.2 57.1 %all-gather.5.cloned.1.call-start = ((), (), s32[]{:S(2)}) async-start(), calls=%async_computation.1 | async-start | bytes 1114112 | tf_op jit(solution)/shard_map/all_gather | solution.py:97
  7.9 247.5 %all-gather.3.cloned.1.call-start = ((), (), s32[]{:S(2)}) async-start(), calls=%async_computation | async-start | bytes 2228224 | tf_op jit(solution)/shard_map/all_gather | solution.py:98
  8.0 197.5 %collective-permute-start = (bf16[2,384,2048]{2,1,0:T(8,128)(2,1)}, bf16[2,384,2048]{2,1,0:T(8,128)(2,1)}, u32[]{:S(2)}, u32[]{:S(2)}) collective-permute-start(bf16[2,384,2048]{2,1,0:T(8,128)(2,1)} %param.9), channel_id=1, source_target_pairs={{0,1},{1,2},{2,3},{3,4},{4,5},{5,6},{6,7},{7,8},{8,9},{9,10},{10,1... | collective-permute-start | bytes 9437192 | tf_op jit(solution)/shard_map/ppermute | solution.py:19
  12.0 193.5 %collective-permute-start.1 = (bf16[2,384,2048]{2,1,0:T(8,128)(2,1)}, bf16[2,384,2048]{2,1,0:T(8,128)(2,1)}, u32[]{:S(2)}, u32[]{:S(2)}) collective-permute-start(bf16[2,384,2048]{2,1,0:T(8,128)(2,1)} %param.9), channel_id=1, source_target_pairs={{1,0},{2,1},{3,2},{4,3},{5,4},{6,5},{7,6},{8,7},{9,8},{10,9},{11,1... | collective-permute-start | bytes 9437192 | tf_op jit(solution)/shard_map/ppermute | solution.py:21
  15.0 270.7 %all-reduce.2.cloned.1.call-start = ((), (), s32[]{:S(2)}) async-start(), calls=%async_computation.2 | async-start | bytes 4194304 | tf_op jit(solution)/shard_map/psum | solution.py:147
  17.3 4.1 %copy-start.9 = (s32[256]{0:T(256)S(1)}, s32[256]{0:T(256)}, u32[]{:S(2)}) copy-start(s32[256]{0:T(256)} %param.12) | copy-start | bytes 3076
  25.8 6.1 %copy-start.3 = (bf16[1,384,2048]{1,2,0:T(8,128)(2,1)S(1)}, bf16[1,384,2048]{1,2,0:T(8,128)(2,1)}, u32[]{:S(2)}) copy-start(bf16[1,384,2048]{1,2,0:T(8,128)(2,1)} %copy.57) | copy-start | bytes 4718596
  28.3 3.6 %copy-start.2 = (f32[16,384,384]{2,1,0:T(8,128)}, f32[16,384,384]{2,1,0:T(8,128)S(1)}, u32[]{:S(2)}) copy-start(f32[16,384,384]{2,1,0:T(8,128)S(1)} %get-tuple-element.26) | copy-start | bytes 28311556
  138.3 4.6 %copy-start.1 = (f32[16,384,256]{2,1,0:T(8,128)S(1)}, f32[16,384,256]{2,1,0:T(8,128)}, u32[]{:S(2)}) copy-start(f32[16,384,256]{2,1,0:T(8,128)} %get-tuple-element.36) | copy-start | bytes 18874372
  237.9 2.7 copy-start.7
  240.6 3.5 %copy-start.5 = (bf16[1,1,384,16,128]{4,3,2,1,0:T(8,128)(2,1)S(1)}, bf16[1,1,384,16,128]{4,3,2,1,0:T(8,128)(2,1)}, u32[]{:S(2)}) copy-start(bf16[1,1,384,16,128]{4,3,2,1,0:T(8,128)(2,1)} %get-tuple-element.14) | copy-start | bytes 4718596
  240.6 5.4 %slice-start = ((s8[9437184]{0:T(1024)(128)(4,1)}), s8[4194304]{0:T(1024)(128)(4,1)S(1)}, s32[]{:S(2)}) async-start(s8[9437184]{0:T(1024)(128)(4,1)} %bitcast.282), calls=%async_computation.3 | async-start | bytes 8388608
  240.6 5.4 %slice-start.1 = ((s8[9437184]{0:T(1024)(128)(4,1)}), s8[1048576]{0:T(1024)(128)(4,1)S(1)}, s32[]{:S(2)}) async-start(s8[9437184]{0:T(1024)(128)(4,1)} %bitcast.282), calls=%async_computation.4 | async-start | bytes 2097152
  244.1 2.2 slice-start.2
  246.3 5.5 %copy-start.6 = (bf16[1,1,384,16,128]{2,4,3,1,0:T(8,128)(2,1)S(1)}, bf16[1,1,384,16,128]{2,4,3,1,0:T(8,128)(2,1)}, u32[]{:S(2)}) copy-start(bf16[1,1,384,16,128]{2,4,3,1,0:T(8,128)(2,1)} %copy.99) | copy-start | bytes 4718596
  274.2 1.8 copy-start.4
  274.2 1.8 copy-start.10
  274.2 2.2 copy-start.11
  274.2 2.7 copy-start.12
  281.4 3.6 %copy-start.8 = (bf16[16,2048]{1,0:T(8,128)(2,1)S(1)}, bf16[16,2048]{1,0:T(8,128)(2,1)}, u32[]{:S(2)}) copy-start(bf16[16,2048]{1,0:T(8,128)(2,1)} %param.10) | copy-start | bytes 196612
Sparse Core Ops, SparseCore 0:
  10.2 54.0 all-gather.4
  66.5 43.8 all-gather.2
  147.5 95.1 all-reduce.1
where the time goes:
time: 299 us; the launch traced here: 298 us
  blocking collectives  125 us (42%)
  local copies, waits for them, and re-layouts  61.2 us (20%)
  matrix products  35.5 us (12%)
  waiting for transfers between devices  29.6 us (10%)
  other arithmetic  26.6 us (9%)
  between operations  14.7 us (5%)
  starting transfers between devices  5.42 us (2%)
    pmax x1, blocking collectives, on_device(): global_max = lax.pmax(maxima, 'rows')  66.7 us
    psum x1, blocking collectives, on_device(): lax.psum((scaled_summed, scaled_totals), 'rows')  58.2 us
    unnamed x38, local copies, waits for them, and re-layouts  29.6 us
    all_gather x1, waiting for transfers between devices, on_device(): lax.all_gather(text_query, 'rows', axis=0, tiled=True)  28.8 us
    slice x2, local copies, waits for them, and re-layouts, on_device(): text_values = text_gathered[1].reshape(-1, head_count, head_width)  12.6 us
    dot_general x3, matrix products, attend_tiles(): jnp.einsum('tqhk,tkhe->tqhe', exponent.astype(jnp.bfloat16), value_rows,...  10.6 us
    dot_general x3, matrix products, attend_rows(): jnp.einsum('qhk,khe->qhe', exponent.astype(jnp.bfloat16), value_rows, pre...  10.5 us
    reduce_sum x2, other arithmetic, attend_tiles(): totals = jnp.sum(exponent, axis=-1)  8.14 us
  transfers between devices with their start and end apart: 5, of which 1 were waited for; matrix products, arithmetic and copies ran while one was open for 38% of the time, Pallas kernels for 0%

commit v1 on v0

--- a/solution.py
+++ b/solution.py
@@ -1,11 +1,41 @@
+import functools
 import math
 import jax
 import jax.numpy as jnp
 from jax import lax
 from jax.sharding import PartitionSpec as P
+from jax.lax import axis_index, axis_size, ppermute
 
 TILE = 384
 masked_score = -1e30
+
+
+def _resolve_stacks_all(field_in, at_axis):
+    b_now, item_now, a_next = (axis_size("rows"), axis_index("rows"), field_in.shape[at_axis])
+    copies = [(num, (num + 1) % b_now) for num in range(b_now)]
+    ledger = [(num, (num - 1) % b_now) for num in range(b_now)]
+    part_next = jnp.zeros(
+        (*field_in.shape[:at_axis], b_now * a_next, *field_in.shape[at_axis + 1 :]), field_in.dtype
+    )
+    part_next = lax.dynamic_update_slice_in_dim(
+        part_next, field_in, item_now * a_next, axis=at_axis
+    )
+    carry_in = far_arr = field_in
+    passed = b_now // 2
+    for j0 in range(1, passed + 1):
+        carry_in = ppermute(carry_in, "rows", copies)
+        part_next = lax.dynamic_update_slice_in_dim(
+            part_next, carry_in, (item_now - j0) % b_now * a_next, axis=at_axis
+        )
+        if j0 < b_now - passed:
+            far_arr = ppermute(far_arr, "rows", ledger)
+            part_next = lax.dynamic_update_slice_in_dim(
+                part_next, far_arr, (item_now + j0) % b_now * a_next, axis=at_axis
+            )
+    return part_next
+
+
+_answer_case = functools.partial(_resolve_stacks_all, at_axis=0)
 
 
 def extended_2(cells, sides, width):
@@ -94,7 +124,7 @@
     reach_back = window_offsets[:, 0]
     reach_ahead = window_offsets[:, 1]
     text_queries, text_gathered = (
-        lax.all_gather(text_query, "rows", axis=0, tiled=True),
+        _answer_case(text_query),
         lax.all_gather(text_pairs, "rows", axis=1, tiled=True),
     )
     text_keys = text_gathered[0].reshape(-1, head_count, head_width)

time: 299 us -> 514 us (1.72); the launches traced: 298 us -> 505 us
  starting transfers between devices: 5.42 us -> 126 us
  local copies, waits for them, and re-layouts: 61.2 us -> 159 us
  waiting for transfers between devices: 29.6 us -> 17.6 us
  matrix products: 35.5 us -> 42.9 us
  blocking collectives: 125 us -> 119 us
    ppermute x0 -> x15, starting transfers between devices: none -> 119 us  [the longest x8 86.1 us: _resolve_stacks_all(): carry_in = ppermute(carry_in, 'rows', copies)]
    dynamic_update_slice x0 -> x16, local copies, waits for them, and re-layouts: none -> 101 us  [the longest x8 48.1 us: _resolve_stacks_all(): lax.dynamic_update_slice_in_dim(part_next, carry_in, (item_now - j0) % b_...]
    all_gather x1 -> x0, waiting for transfers between devices: 28.8 us -> none  [on_device(): lax.all_gather(text_query, 'rows', axis=0, tiled=True)]
    ppermute x0 -> x15, waiting for transfers between devices: none -> 17.5 us  [the longest x8 11.3 us: _resolve_stacks_all(): carry_in = ppermute(carry_in, 'rows', copies)]
    pmax x1, blocking collectives: 66.7 us -> 60 us  [on_device(): global_max = lax.pmax(maxima, 'rows')]
    unnamed x38 -> x43, local copies, waits for them, and re-layouts: 29.6 us -> 27.1 us
  transfers between devices with their start and end apart: 5 -> 19, of which waited for: 1 -> 5; matrix products, arithmetic and copies ran while one was open for 38% -> 43% of each run, Pallas kernels for 0% -> 0%
where the time goes in v1:
time: 514 us; the launch traced here: 505 us
  local copies, waits for them, and re-layouts  159 us (31%)
  starting transfers between devices  126 us (25%)
  blocking collectives  119 us (23%)
  matrix products  42.9 us (8%)
  other arithmetic  25.9 us (5%)
  waiting for transfers between devices  17.6 us (3%)
  between operations  15.3 us (3%)
    ppermute x8, starting transfers between devices, _resolve_stacks_all(): carry_in = ppermute(carry_in, 'rows', copies)  86.1 us
    pmax x1, blocking collectives, on_device(): global_max = lax.pmax(maxima, 'rows')  60 us
    psum x1, blocking collectives, on_device(): lax.psum((scaled_summed, scaled_totals), 'rows')  58.8 us
    dynamic_update_slice x8, local copies, waits for them, and re-layouts, _resolve_stacks_all(): lax.dynamic_update_slice_in_dim(part_next, carry_in, (item_now - j0) % b_...  48.1 us
    dynamic_update_slice x7, local copies, waits for them, and re-layouts, _resolve_stacks_all(): lax.dynamic_update_slice_in_dim(part_next, far_arr, (item_now + j0) % b_n...  47.4 us
    ppermute x7, starting transfers between devices, _resolve_stacks_all(): far_arr = ppermute(far_arr, 'rows', ledger)  32.6 us
    unnamed x43, local copies, waits for them, and re-layouts  27.1 us
    dot_general x3, matrix products, attend_tiles(): jnp.einsum('tqhk,tkhe->tqhe', exponent.astype(jnp.bfloat16), value_rows,...  14.9 us
  transfers between devices with their start and end apart: 19, of which 5 were waited for; matrix products, arithmetic and copies ran while one was open for 43% of the time, Pallas kernels for 0%

profile of v1, /device:TPU:0, one launch (start us, length us, event | category | flops | bytes accessed | tf_op | source)
XLA Modules:
  0.0 505.3 jit_solution(1659386276427971232)
XLA Ops:
  9.0 5.1 %collective-permute-start.3 = (bf16[16,2048]{0,1:T(8,128)(2,1)S(1)}, bf16[16,2048]{0,1:T(8,128)(2,1)S(1)}, u32[]{:S(2)}, u32[]{:S(2)}) collective-permute-start(bf16[16,2048]{0,1:T(8,128)(2,1)S(1)} %copy.74), channel_id=1, source_target_pairs={{0,15},{1,0},{2,1},{3,2},{4,3},{5,4},{6,5},{7,6},{8,7},{9,8},{10,9... | collective-permute-start | bytes 196616 | tf_op jit(solution)/shard_map/ppermute | solution.py:31
  14.0 6.9 %collective-permute-done.2 = bf16[16,2048]{0,1:T(8,128)(2,1)S(1)} collective-permute-done((bf16[16,2048]{0,1:T(8,128)(2,1)S(1)}, bf16[16,2048]{0,1:T(8,128)(2,1)S(1)}, u32[]{:S(2)}, u32[]{:S(2)}) %collective-permute-start.2) | collective-permute-done | bytes 65568 | tf_op jit(solution)/shard_map/ppermute | solution.py:26
  20.9 2.4 collective-permute-start.4
  23.3 6.0 %collective-permute-start = (bf16[2,384,2048]{2,1,0:T(8,128)(2,1)}, bf16[2,384,2048]{2,1,0:T(8,128)(2,1)}, u32[]{:S(2)}, u32[]{:S(2)}) collective-permute-start(bf16[2,384,2048]{2,1,0:T(8,128)(2,1)} %param.9), channel_id=1, source_target_pairs={{0,1},{1,2},{2,3},{3,4},{4,5},{5,6},{6,7},{7,8},{8,9},{9,10},{10,1... | collective-permute-start | bytes 9437192 | tf_op jit(solution)/shard_map/ppermute | solution.py:49
  29.4 1.3 collective-permute-start.1
  30.7 1.7 copy.59
  32.5 3.8 collective-permute-start.5
  36.2 4.0 fusion.134
  40.3 4.0 collective-permute-done.5
  44.3 17.0 %collective-permute-start.7 = (bf16[16,2048]{0,1:T(8,128)(2,1)}, bf16[16,2048]{0,1:T(8,128)(2,1)}, u32[]{:S(2)}, u32[]{:S(2)}) collective-permute-start(bf16[16,2048]{0,1:T(8,128)(2,1)} %collective-permute-done.5), channel_id=1, source_target_pairs={{0,15},{1,0},{2,1},{3,2},{4,3},{5,4},{6,5},{7,6},{8,7},{9,8},{10,9... | collective-permute-start | bytes 196616 | tf_op jit(solution)/shard_map/ppermute | solution.py:31
  61.3 3.5 collective-permute-done.6
  64.8 58.5 %collective-permute-start.8 = (bf16[16,2048]{0,1:T(8,128)(2,1)}, bf16[16,2048]{0,1:T(8,128)(2,1)}, u32[]{:S(2)}, u32[]{:S(2)}) collective-permute-start(bf16[16,2048]{0,1:T(8,128)(2,1)} %collective-permute-done.6), channel_id=1, source_target_pairs={{0,1},{1,2},{2,3},{3,4},{4,5},{5,6},{6,7},{7,8},{8,9},{9,10},{10,1... | collective-permute-start | bytes 196616 | tf_op jit(solution)/shard_map/ppermute | solution.py:26
  123.4 1.9 copy.95
  126.3 11.6 %collective-permute-start.10 = (bf16[16,2048]{0,1:T(8,128)(2,1)}, bf16[16,2048]{0,1:T(8,128)(2,1)}, u32[]{:S(2)}, u32[]{:S(2)}) collective-permute-start(bf16[16,2048]{0,1:T(8,128)(2,1)} %collective-permute-done.8), channel_id=1, source_target_pairs={{0,1},{1,2},{2,3},{3,4},{4,5},{5,6},{6,7},{7,8},{8,9},{9,10},{10,1... | collective-permute-start | bytes 196616 | tf_op jit(solution)/shard_map/ppermute | solution.py:26
  137.9 6.0 %bitcast_reduce_fusion.2 = (f32[384,16]{0,1:T(8,128)S(1)}, f32[16,384,384]{2,1,0:T(8,128)}) fusion(pred[16]{0:T(512)(128)(4,1)S(1)} %get-tuple-element.24, bf16[384,16,128]{0,2,1:T(8,128)(2,1)S(1)} %bitcast.286, bf16[384,2048]{1,0:T(8,128)(2,1)S(1)} %copy-done), kind=kOutput, calls=%fused_computation.12 | convolution fusion | flops 611051520 | bytes 12607504 | tf_op jit(solution)/shard_map/tqhe,tkhe->tqhk/dot_general | solution.py:60
  143.9 2.6 copy.57
  146.5 2.5 collective-permute-start.12
  149.0 7.7 %fusion.67 = bf16[16,384,128]{1,2,0:T(8,128)(2,1)} fusion(bf16[384,16,128]{0,2,1:T(8,128)(2,1)} %bitcast.290, f32[16,384,384]{2,1,0:T(8,128)} %get-tuple-element.26, f32[384,16]{0,1:T(8,128)S(1)} %get-tuple-element.25, pred[16]{0:T(512)(128)(4,1)S(1)} %get-tuple-element.24), kind=kOutput, calls=%fused_computation.81 | convolution fusion | flops 616562688 | bytes 12607504 | tf_op jit(solution)/shard_map/tqhk,tkhe->tqhe/dot_general | solution.py:67
  157.4 2.0 collective-permute-start.13
  159.4 4.1 collective-permute-start.14
  164.3 2.1 collective-permute-done.13
  166.5 4.7 collective-permute-start.15
  171.2 6.4 %collective-permute-start.16 = (bf16[16,2048]{0,1:T(8,128)(2,1)}, bf16[16,2048]{0,1:T(8,128)(2,1)}, u32[]{:S(2)}, u32[]{:S(2)}) collective-permute-start(bf16[16,2048]{0,1:T(8,128)(2,1)} %collective-permute-done.14), channel_id=1, source_target_pairs={{0,1},{1,2},{2,3},{3,4},{4,5},{5,6},{6,7},{7,8},{8,9},{9,10},{10,1... | collective-permute-start | bytes 196616 | tf_op jit(solution)/shard_map/ppermute | solution.py:26
  178.7 6.0 %dynamic_update_slice.48 = bf16[256,2048]{0,1:T(8,128)(2,1)} dynamic-update-slice(bf16[256,2048]{0,1:T(8,128)(2,1)} %broadcast_in_dim.137, bf16[16,2048]{0,1:T(8,128)(2,1)} %copy-done.3, s32[]{:T(128)S(6)} %select_n.182, s32[]{:T(128)} %constant.117.clone.1) | dynamic-update-slice | bytes 131076 | tf_op jit(solution)/shard_map/dynamic_update_slice | solution.py:20
  184.6 6.1 %dynamic_update_slice.49 = bf16[256,2048]{0,1:T(8,128)(2,1)} dynamic-update-slice(bf16[256,2048]{0,1:T(8,128)(2,1)} %dynamic_update_slice.48, bf16[16,2048]{0,1:T(8,128)(2,1)} %copy-done.7, s32[]{:T(128)S(6)} %select_n.184, s32[]{:T(128)} %constant.117.clone.1) | dynamic-update-slice | bytes 131076 | tf_op jit(solution)/shard_map/dynamic_update_slice | solution.py:27
  190.7 6.8 %dynamic_update_slice.50 = bf16[256,2048]{0,1:T(8,128)(2,1)} dynamic-update-slice(bf16[256,2048]{0,1:T(8,128)(2,1)} %dynamic_update_slice.49, bf16[16,2048]{0,1:T(8,128)(2,1)} %copy-done.8, s32[]{:T(128)S(6)} %select_n.186, s32[]{:T(128)} %constant.117.clone.1) | dynamic-update-slice | bytes 131076 | tf_op jit(solution)/shard_map/dynamic_update_slice | solution.py:32
  197.5 6.1 %dynamic_update_slice.51 = bf16[256,2048]{0,1:T(8,128)(2,1)} dynamic-update-slice(bf16[256,2048]{0,1:T(8,128)(2,1)} %dynamic_update_slice.50, bf16[16,2048]{0,1:T(8,128)(2,1)} %collective-permute-done.4, s32[]{:T(128)S(6)} %select_n.188, s32[]{:T(128)} %constant.117.clone.1) | dynamic-update-slice | bytes 131076 | tf_op jit(solution)/shard_map/dynamic_update_slice | solution.py:27
  203.6 6.8 %dynamic_update_slice.52 = bf16[256,2048]{0,1:T(8,128)(2,1)} dynamic-update-slice(bf16[256,2048]{0,1:T(8,128)(2,1)} %dynamic_update_slice.51, bf16[16,2048]{0,1:T(8,128)(2,1)} %collective-permute-done.5, s32[]{:T(128)S(6)} %select_n.190, s32[]{:T(128)} %constant.117.clone.1) | dynamic-update-slice | bytes 131076 | tf_op jit(solution)/shard_map/dynamic_update_slice | solution.py:32
  210.4 6.1 %dynamic_update_slice.53 = bf16[256,2048]{0,1:T(8,128)(2,1)} dynamic-update-slice(bf16[256,2048]{0,1:T(8,128)(2,1)} %dynamic_update_slice.52, bf16[16,2048]{0,1:T(8,128)(2,1)} %collective-permute-done.6, s32[]{:T(128)S(6)} %select_n.192, s32[]{:T(128)} %constant.117.clone.1) | dynamic-update-slice | bytes 131076 | tf_op jit(solution)/shard_map/dynamic_update_slice | solution.py:27
  216.5 6.8 %dynamic_update_slice.54 = bf16[256,2048]{0,1:T(8,128)(2,1)} dynamic-update-slice(bf16[256,2048]{0,1:T(8,128)(2,1)} %dynamic_update_slice.53, bf16[16,2048]{0,1:T(8,128)(2,1)} %collective-permute-done.7, s32[]{:T(128)S(6)} %select_n.194, s32[]{:T(128)} %constant.117.clone.1) | dynamic-update-slice | bytes 131076 | tf_op jit(solution)/shard_map/dynamic_update_slice | solution.py:32
  223.3 6.1 %dynamic_update_slice.55 = bf16[256,2048]{0,1:T(8,128)(2,1)} dynamic-update-slice(bf16[256,2048]{0,1:T(8,128)(2,1)} %dynamic_update_slice.54, bf16[16,2048]{0,1:T(8,128)(2,1)} %collective-permute-done.8, s32[]{:T(128)S(6)} %select_n.196, s32[]{:T(128)} %constant.117.clone.1) | dynamic-update-slice | bytes 131076 | tf_op jit(solution)/shard_map/dynamic_update_slice | solution.py:27
  229.4 6.8 %dynamic_update_slice.56 = bf16[256,2048]{0,1:T(8,128)(2,1)} dynamic-update-slice(bf16[256,2048]{0,1:T(8,128)(2,1)} %dynamic_update_slice.55, bf16[16,2048]{0,1:T(8,128)(2,1)} %collective-permute-done.9, s32[]{:T(128)S(6)} %select_n.198, s32[]{:T(128)} %constant.117.clone.1) | dynamic-update-slice | bytes 131076 | tf_op jit(solution)/shard_map/dynamic_update_slice | solution.py:32
  236.1 6.1 %dynamic_update_slice.57 = bf16[256,2048]{0,1:T(8,128)(2,1)} dynamic-update-slice(bf16[256,2048]{0,1:T(8,128)(2,1)} %dynamic_update_slice.56, bf16[16,2048]{0,1:T(8,128)(2,1)} %collective-permute-done.10, s32[]{:T(128)S(6)} %select_n.200, s32[]{:T(128)} %constant.117.clone.1) | dynamic-update-slice | bytes 131076 | tf_op jit(solution)/shard_map/dynamic_update_slice | solution.py:27
  242.3 6.8 %dynamic_update_slice.58 = bf16[256,2048]{0,1:T(8,128)(2,1)} dynamic-update-slice(bf16[256,2048]{0,1:T(8,128)(2,1)} %dynamic_update_slice.57, bf16[16,2048]{0,1:T(8,128)(2,1)} %collective-permute-done.11, s32[]{:T(128)S(6)} %select_n.202, s32[]{:T(128)} %constant.117.clone.1) | dynamic-update-slice | bytes 131076 | tf_op jit(solution)/shard_map/dynamic_update_slice | solution.py:32
  249.0 6.1 %dynamic_update_slice.59 = bf16[256,2048]{0,1:T(8,128)(2,1)} dynamic-update-slice(bf16[256,2048]{0,1:T(8,128)(2,1)} %dynamic_update_slice.58, bf16[16,2048]{0,1:T(8,128)(2,1)} %collective-permute-done.12, s32[]{:T(128)S(6)} %select_n.204, s32[]{:T(128)} %constant.117.clone.1) | dynamic-update-slice | bytes 131076 | tf_op jit(solution)/shard_map/dynamic_update_slice | solution.py:27
  255.1 6.8 %dynamic_update_slice.60 = bf16[256,2048]{0,1:T(8,128)(2,1)} dynamic-update-slice(bf16[256,2048]{0,1:T(8,128)(2,1)} %dynamic_update_slice.59, bf16[16,2048]{0,1:T(8,128)(2,1)} %collective-permute-done.13, s32[]{:T(128)S(6)} %select_n.206, s32[]{:T(128)} %constant.117.clone.1) | dynamic-update-slice | bytes 131076 | tf_op jit(solution)/shard_map/dynamic_update_slice | solution.py:32
  261.9 6.1 %dynamic_update_slice.61 = bf16[256,2048]{0,1:T(8,128)(2,1)} dynamic-update-slice(bf16[256,2048]{0,1:T(8,128)(2,1)} %dynamic_update_slice.60, bf16[16,2048]{0,1:T(8,128)(2,1)} %collective-permute-done.14, s32[]{:T(128)S(6)} %select_n.208, s32[]{:T(128)} %constant.117.clone.1) | dynamic-update-slice | bytes 131076 | tf_op jit(solution)/shard_map/dynamic_update_slice | solution.py:27
  268.0 6.8 %dynamic_update_slice.62 = bf16[256,2048]{0,1:T(8,128)(2,1)} dynamic-update-slice(bf16[256,2048]{0,1:T(8,128)(2,1)} %dynamic_update_slice.61, bf16[16,2048]{0,1:T(8,128)(2,1)} %collective-permute-done.15, s32[]{:T(128)S(6)} %select_n.210, s32[]{:T(128)} %constant.117.clone.1) | dynamic-update-slice | bytes 131076 | tf_op jit(solution)/shard_map/dynamic_update_slice | solution.py:32
  274.8 5.3 %dynamic_update_slice.63 = bf16[256,2048]{0,1:T(8,128)(2,1)} dynamic-update-slice(bf16[256,2048]{0,1:T(8,128)(2,1)} %dynamic_update_slice.62, bf16[16,2048]{0,1:T(8,128)(2,1)} %collective-permute-done.16, s32[]{:T(128)S(6)} %select_n.212, s32[]{:T(128)} %constant.117.clone.1) | dynamic-update-slice | bytes 131076 | tf_op jit(solution)/shard_map/dynamic_update_slice | solution.py:27
  280.1 4.9 bitcast_reduce_fusion.3
  285.0 60.0 %pmax.7 = f32[256,16]{0,1:T(8,128)S(1)} all-reduce(f32[256,16]{0,1:T(8,128)S(1)} %get-tuple-element.35), channel_id=1, replica_groups=mesh['groups'=2,'rows'=16] {'rows'}, use_global_device_ids=true, to_apply=%region_9.10 | all-reduce | flops 4096 | bytes 32768 | tf_op jit(solution)/shard_map/pmax | solution.py:173
  345.0 4.1 fusion.15
  349.7 3.9 bitcast_multiply_fusion.2
  353.6 58.8 %psum.15 = f32[256,16]{0,1:T(8,128)S(1)} all-reduce(f32[256,16]{0,1:T(8,128)S(1)} %get-tuple-element.5), channel_id=1, replica_groups=mesh['groups'=2,'rows'=16] {'rows'}, use_global_device_ids=true, to_apply=%region_13.14 | all-reduce | flops 4096 | bytes 32768 | tf_op jit(solution)/shard_map/psum | solution.py:177
  412.3 7.6 %pad_maximum_fusion = bf16[2,1152,2048]{2,1,0:T(8,128)(2,1)} fusion(bf16[2,384,2048]{2,1,0:T(8,128)(2,1)} %collective-permute-done.1, bf16[2,384,2048]{2,1,0:T(8,128)(2,1)} %param.9, bf16[2,384,2048]{2,1,0:T(8,128)(2,1)} %collective-permute-done), kind=kLoop, calls=%fused_computation | loop fusion | flops 28311552 | bytes 18874368 | tf_op jit(solution)/shard_map/concatenate | solution.py:47
  420.0 11.1 %copy.104 = bf16[288,8,16,128]{3,2,1,0:T(8,128)(2,1)} copy(bf16[288,8,16,128]{3,1,2,0:T(8,128)(2,1)} %bitcast.284) | data formatting | bytes 18874368
  431.0 5.6 %fusion.133 = (bf16[1,1,384,16,128]{4,3,2,1,0:T(8,128)(2,1)}, bf16[1,1,384,16,128]{4,3,2,1,0:T(8,128)(2,1)}, bf16[1,1,384,16,128]{4,3,2,1,0:T(8,128)(2,1)}, bf16[1,1,384,16,128]{4,3,2,1,0:T(8,128)(2,1)S(1)}) fusion(bf16[2,3,384,16,128]{4,3,2,1,0:T(8,128)(2,1)} %bitcast.285), kind=kLoop, calls=%fused_computation.154 | loop fusion | bytes 12582912 | tf_op jit(solution)/shard_map/slice | solution.py:158
  436.6 2.8 copy.99
  439.5 2.0 copy.100
  441.5 3.3 bitcast_reduce_fusion
  444.8 2.7 fusion.10
  447.5 3.6 fusion.73
  451.2 1.9 bitcast_reduce_fusion.1
  453.4 5.5 %fusion.6 = (f32[384,16]{0,1:T(8,128)S(1)}, f32[384,16]{0,1:T(8,128)S(1)}) fusion(f32[16,384,384]{2,1,0:T(8,128)S(1)} %bitcast.283, f32[384,16]{0,1:T(8,128)S(1)} %get-tuple-element.25, pred[16]{0:T(512)(128)(4,1)S(1)} %get-tuple-element.24, f32[384,16]{0,1:T(8,128)S(1)} %get-tuple-element.29, f32[16,384,384]{2,1,0:T(8,128)S(1)} %get-tuple-element.30, ...), kind=kLoop, calls=%fused_computation.16 | loop fusion | flops 23580672 | bytes 18972704 | tf_op jit(solution)/shard_map/reduce_sum | solution.py:66
  458.9 3.6 fusion.70
  462.4 6.8 %fusion.135 = (bf16[1,256,2048]{2,0,1:T(2,128)(2,1)}, bf16[1,256,2048]{2,0,1:T(2,128)(2,1)}) fusion(bf16[2,256,2048]{2,0,1:T(2,128)(2,1)} %all-gather.2.cloned.1.call-done), kind=kLoop, calls=%fused_computation.156 | loop fusion | bytes 4194304 | tf_op jit(solution)/shard_map/slice | solution.py:131
  469.2 5.8 %copy.67 = bf16[1,256,2048]{1,2,0:T(8,128)(2,1)} copy(bf16[1,256,2048]{2,0,1:T(2,128)(2,1)} %get-tuple-element.18) | data formatting | bytes 2097152 | tf_op jit(solution)/shard_map/slice | solution.py:131
  475.0 4.7 copy.96
  479.7 1.4 bitcast_reduce_fusion.4
  481.2 1.7 fusion.44
  483.8 4.5 fusion.52
  488.3 3.6 copy.73
  492.6 1.7 fusion.98
  494.9 3.4 multiply_convert_fusion
  (71 shorter events, 7.8 us)
Async XLA Ops:
  7.2 130.7 %copy-start = (bf16[384,2048]{1,0:T(8,128)(2,1)S(1)}, bf16[384,2048]{1,0:T(8,128)(2,1)}, u32[]{:S(2)}) copy-start(bf16[384,2048]{1,0:T(8,128)(2,1)} %param.8) | copy-start | bytes 4718596
  7.2 455.2 %all-gather.2.cloned.1.call-start = ((), (), s32[]{:S(2)}) async-start(), calls=%async_computation | async-start | bytes 2228224 | tf_op jit(solution)/shard_map/all_gather | solution.py:128
  8.5 31.8 %copy-start.3 = (bf16[16,2048]{0,1:T(8,128)(2,1)}, bf16[16,2048]{0,1:T(8,128)(2,1)S(1)}, u32[]{:S(2)}) copy-start(bf16[16,2048]{0,1:T(8,128)(2,1)S(1)} %copy.74) | copy-start | bytes 196612
  8.5 12.5 %collective-permute-start.2 = (bf16[16,2048]{0,1:T(8,128)(2,1)S(1)}, bf16[16,2048]{0,1:T(8,128)(2,1)S(1)}, u32[]{:S(2)}, u32[]{:S(2)}) collective-permute-start(bf16[16,2048]{0,1:T(8,128)(2,1)S(1)} %copy.74), channel_id=1, source_target_pairs={{0,1},{1,2},{2,3},{3,4},{4,5},{5,6},{6,7},{7,8},{8,9},{9,10},{10,1... | collective-permute-start | bytes 196616 | tf_op jit(solution)/shard_map/ppermute | solution.py:26
  9.0 23.5 %collective-permute-start.3 = (bf16[16,2048]{0,1:T(8,128)(2,1)S(1)}, bf16[16,2048]{0,1:T(8,128)(2,1)S(1)}, u32[]{:S(2)}, u32[]{:S(2)}) collective-permute-start(bf16[16,2048]{0,1:T(8,128)(2,1)S(1)} %copy.74), channel_id=1, source_target_pairs={{0,15},{1,0},{2,1},{3,2},{4,3},{5,4},{6,5},{7,6},{8,7},{9,8},{10,9... | collective-permute-start | bytes 196616 | tf_op jit(solution)/shard_map/ppermute | solution.py:31
  20.9 19.3 %copy-start.7 = (bf16[16,2048]{0,1:T(8,128)(2,1)}, bf16[16,2048]{0,1:T(8,128)(2,1)S(1)}, u32[]{:S(2)}) copy-start(bf16[16,2048]{0,1:T(8,128)(2,1)S(1)} %collective-permute-done.2) | copy-start | bytes 196612
  20.9 15.3 %collective-permute-start.4 = (bf16[16,2048]{0,1:T(8,128)(2,1)S(1)}, bf16[16,2048]{0,1:T(8,128)(2,1)}, u32[]{:S(2)}, u32[]{:S(2)}) collective-permute-start(bf16[16,2048]{0,1:T(8,128)(2,1)S(1)} %collective-permute-done.2), channel_id=1, source_target_pairs={{0,1},{1,2},{2,3},{3,4},{4,5},{5,6},{6,7},{7,8},{8,9},{9,10},{10,1... | collective-permute-start | bytes 196616 | tf_op jit(solution)/shard_map/ppermute | solution.py:26
  23.3 389.0 %collective-permute-start = (bf16[2,384,2048]{2,1,0:T(8,128)(2,1)}, bf16[2,384,2048]{2,1,0:T(8,128)(2,1)}, u32[]{:S(2)}, u32[]{:S(2)}) collective-permute-start(bf16[2,384,2048]{2,1,0:T(8,128)(2,1)} %param.9), channel_id=1, source_target_pairs={{0,1},{1,2},{2,3},{3,4},{4,5},{5,6},{6,7},{7,8},{8,9},{9,10},{10,1... | collective-permute-start | bytes 9437192 | tf_op jit(solution)/shard_map/ppermute | solution.py:49
  29.4 383.0 %collective-permute-start.1 = (bf16[2,384,2048]{2,1,0:T(8,128)(2,1)}, bf16[2,384,2048]{2,1,0:T(8,128)(2,1)}, u32[]{:S(2)}, u32[]{:S(2)}) collective-permute-start(bf16[2,384,2048]{2,1,0:T(8,128)(2,1)} %param.9), channel_id=1, source_target_pairs={{1,0},{2,1},{3,2},{4,3},{5,4},{6,5},{7,6},{8,7},{9,8},{10,9},{11,1... | collective-permute-start | bytes 9437192 | tf_op jit(solution)/shard_map/ppermute | solution.py:51
  32.4 91.0 %copy-start.10 = (s32[16,2]{0,1:T(2,128)S(1)}, s32[16,2]{0,1:T(2,128)}, u32[]{:S(2)}) copy-start(s32[16,2]{0,1:T(2,128)} %param.13) | copy-start | bytes 388
  32.4 460.2 %all-reduce.2.cloned.1.call-start = ((), (), s32[]{:S(2)}) async-start(), calls=%async_computation.1 | async-start | bytes 4194304 | tf_op jit(solution)/shard_map/psum | solution.py:177
  32.5 7.8 %copy-start.8 = (bf16[16,2048]{0,1:T(8,128)(2,1)}, bf16[16,2048]{0,1:T(8,128)(2,1)S(1)}, u32[]{:S(2)}) copy-start(bf16[16,2048]{0,1:T(8,128)(2,1)S(1)} %collective-permute-done.3) | copy-start | bytes 196612
  32.5 11.9 %collective-permute-start.5 = (bf16[16,2048]{0,1:T(8,128)(2,1)S(1)}, bf16[16,2048]{0,1:T(8,128)(2,1)}, u32[]{:S(2)}, u32[]{:S(2)}) collective-permute-start(bf16[16,2048]{0,1:T(8,128)(2,1)S(1)} %collective-permute-done.3), channel_id=1, source_target_pairs={{0,15},{1,0},{2,1},{3,2},{4,3},{5,4},{6,5},{7,6},{8,7},{9,8},{10,9... | collective-permute-start | bytes 196616 | tf_op jit(solution)/shard_map/ppermute | solution.py:31
  36.2 28.6 %collective-permute-start.6 = (bf16[16,2048]{0,1:T(8,128)(2,1)}, bf16[16,2048]{0,1:T(8,128)(2,1)}, u32[]{:S(2)}, u32[]{:S(2)}) collective-permute-start(bf16[16,2048]{0,1:T(8,128)(2,1)} %collective-permute-done.4), channel_id=1, source_target_pairs={{0,1},{1,2},{2,3},{3,4},{4,5},{5,6},{6,7},{7,8},{8,9},{9,10},{10,1... | collective-permute-start | bytes 196616 | tf_op jit(solution)/shard_map/ppermute | solution.py:26
  44.3 80.9 %collective-permute-start.7 = (bf16[16,2048]{0,1:T(8,128)(2,1)}, bf16[16,2048]{0,1:T(8,128)(2,1)}, u32[]{:S(2)}, u32[]{:S(2)}) collective-permute-start(bf16[16,2048]{0,1:T(8,128)(2,1)} %collective-permute-done.5), channel_id=1, source_target_pairs={{0,15},{1,0},{2,1},{3,2},{4,3},{5,4},{6,5},{7,6},{8,7},{9,8},{10,9... | collective-permute-start | bytes 196616 | tf_op jit(solution)/shard_map/ppermute | solution.py:31
  64.8 61.5 %collective-permute-start.8 = (bf16[16,2048]{0,1:T(8,128)(2,1)}, bf16[16,2048]{0,1:T(8,128)(2,1)}, u32[]{:S(2)}, u32[]{:S(2)}) collective-permute-start(bf16[16,2048]{0,1:T(8,128)(2,1)} %collective-permute-done.6), channel_id=1, source_target_pairs={{0,1},{1,2},{2,3},{3,4},{4,5},{5,6},{6,7},{7,8},{8,9},{9,10},{10,1... | collective-permute-start | bytes 196616 | tf_op jit(solution)/shard_map/ppermute | solution.py:26
  125.2 21.2 %collective-permute-start.9 = (bf16[16,2048]{0,1:T(8,128)(2,1)}, bf16[16,2048]{0,1:T(8,128)(2,1)}, u32[]{:S(2)}, u32[]{:S(2)}) collective-permute-start(bf16[16,2048]{0,1:T(8,128)(2,1)} %collective-permute-done.7), channel_id=1, source_target_pairs={{0,15},{1,0},{2,1},{3,2},{4,3},{5,4},{6,5},{7,6},{8,7},{9,8},{10,9... | collective-permute-start | bytes 196616 | tf_op jit(solution)/shard_map/ppermute | solution.py:31
  126.3 20.2 %collective-permute-start.10 = (bf16[16,2048]{0,1:T(8,128)(2,1)}, bf16[16,2048]{0,1:T(8,128)(2,1)}, u32[]{:S(2)}, u32[]{:S(2)}) collective-permute-start(bf16[16,2048]{0,1:T(8,128)(2,1)} %collective-permute-done.8), channel_id=1, source_target_pairs={{0,1},{1,2},{2,3},{3,4},{4,5},{5,6},{6,7},{7,8},{8,9},{9,10},{10,1... | collective-permute-start | bytes 196616 | tf_op jit(solution)/shard_map/ppermute | solution.py:26
  146.5 10.9 %collective-permute-start.11 = (bf16[16,2048]{0,1:T(8,128)(2,1)}, bf16[16,2048]{0,1:T(8,128)(2,1)}, u32[]{:S(2)}, u32[]{:S(2)}) collective-permute-start(bf16[16,2048]{0,1:T(8,128)(2,1)} %collective-permute-done.9), channel_id=1, source_target_pairs={{0,15},{1,0},{2,1},{3,2},{4,3},{5,4},{6,5},{7,6},{8,7},{9,8},{10,9... | collective-permute-start | bytes 196616 | tf_op jit(solution)/shard_map/ppermute | solution.py:31
  146.5 12.9 %collective-permute-start.12 = (bf16[16,2048]{0,1:T(8,128)(2,1)}, bf16[16,2048]{0,1:T(8,128)(2,1)}, u32[]{:S(2)}, u32[]{:S(2)}) collective-permute-start(bf16[16,2048]{0,1:T(8,128)(2,1)} %collective-permute-done.10), channel_id=1, source_target_pairs={{0,1},{1,2},{2,3},{3,4},{4,5},{5,6},{6,7},{7,8},{8,9},{9,10},{10,1... | collective-permute-start | bytes 196616 | tf_op jit(solution)/shard_map/ppermute | solution.py:26
  149.0 28.6 %copy-start.11 = (s32[256]{0:T(256)S(1)}, s32[256]{0:T(256)}, u32[]{:S(2)}) copy-start(s32[256]{0:T(256)} %param.12) | copy-start | bytes 3076
  157.4 9.0 %collective-permute-start.13 = (bf16[16,2048]{0,1:T(8,128)(2,1)}, bf16[16,2048]{0,1:T(8,128)(2,1)}, u32[]{:S(2)}, u32[]{:S(2)}) collective-permute-start(bf16[16,2048]{0,1:T(8,128)(2,1)} %collective-permute-done.11), channel_id=1, source_target_pairs={{0,15},{1,0},{2,1},{3,2},{4,3},{5,4},{6,5},{7,6},{8,7},{9,8},{10,9... | collective-permute-start | bytes 196616 | tf_op jit(solution)/shard_map/ppermute | solution.py:31
  159.4 11.7 %collective-permute-start.14 = (bf16[16,2048]{0,1:T(8,128)(2,1)}, bf16[16,2048]{0,1:T(8,128)(2,1)}, u32[]{:S(2)}, u32[]{:S(2)}) collective-permute-start(bf16[16,2048]{0,1:T(8,128)(2,1)} %collective-permute-done.12), channel_id=1, source_target_pairs={{0,1},{1,2},{2,3},{3,4},{4,5},{5,6},{6,7},{7,8},{8,9},{9,10},{10,1... | collective-permute-start | bytes 196616 | tf_op jit(solution)/shard_map/ppermute | solution.py:26
  166.5 101.6 %collective-permute-start.15 = (bf16[16,2048]{0,1:T(8,128)(2,1)}, bf16[16,2048]{0,1:T(8,128)(2,1)}, u32[]{:S(2)}, u32[]{:S(2)}) collective-permute-start(bf16[16,2048]{0,1:T(8,128)(2,1)} %collective-permute-done.13), channel_id=1, source_target_pairs={{0,15},{1,0},{2,1},{3,2},{4,3},{5,4},{6,5},{7,6},{8,7},{9,8},{10,9... | collective-permute-start | bytes 196616 | tf_op jit(solution)/shard_map/ppermute | solution.py:31
  171.2 103.6 %collective-permute-start.16 = (bf16[16,2048]{0,1:T(8,128)(2,1)}, bf16[16,2048]{0,1:T(8,128)(2,1)}, u32[]{:S(2)}, u32[]{:S(2)}) collective-permute-start(bf16[16,2048]{0,1:T(8,128)(2,1)} %collective-permute-done.14), channel_id=1, source_target_pairs={{0,1},{1,2},{2,3},{3,4},{4,5},{5,6},{6,7},{7,8},{8,9},{9,10},{10,1... | collective-permute-start | bytes 196616 | tf_op jit(solution)/shard_map/ppermute | solution.py:26
  345.0 4.6 copy-start.1
  444.8 2.7 copy-start.6
  447.5 3.7 copy-start.4
  447.5 5.6 %slice-start = ((s8[9437184]{0:T(1024)(128)(4,1)}), s8[4194304]{0:T(1024)(128)(4,1)S(1)}, s32[]{:S(2)}) async-start(s8[9437184]{0:T(1024)(128)(4,1)} %bitcast.282), calls=%async_computation.2 | async-start | bytes 8388608
  447.5 5.6 %slice-start.1 = ((s8[9437184]{0:T(1024)(128)(4,1)}), s8[1048576]{0:T(1024)(128)(4,1)S(1)}, s32[]{:S(2)}) async-start(s8[9437184]{0:T(1024)(128)(4,1)} %bitcast.282), calls=%async_computation.3 | async-start | bytes 2097152
  451.2 2.2 slice-start.2
  453.4 5.5 %copy-start.5 = (bf16[1,1,384,16,128]{2,4,3,1,0:T(8,128)(2,1)S(1)}, bf16[1,1,384,16,128]{2,4,3,1,0:T(8,128)(2,1)}, u32[]{:S(2)}) copy-start(bf16[1,1,384,16,128]{2,4,3,1,0:T(8,128)(2,1)} %copy.99) | copy-start | bytes 4718596
  481.1 1.8 copy-start.2
  481.2 1.8 copy-start.12
  481.2 2.2 copy-start.13
  481.2 2.7 copy-start.14
  488.3 3.6 copy-start.9
Sparse Core Ops, SparseCore 0:
  32.5 57.2 all-gather.1
  353.7 95.2 all-reduce.1
